TPU v7x, 128 devices: a whole 4x4x4 slice. The times are simulated.
128 devices in a mesh: gx: 16 (over z, x), gy: 8 (over y, core).
Axes of the slice: x: 4, y: 4, z: 4, core: 2. Of those that a mesh axis runs over, the one named last changes fastest.
Arguments:
- fields: float32 [5, 768, 512, 128], P(None, 'gx', 'gy'), may hold values from -6 to 9
- emission: float32 [16, 128, 4, 128], P('gx', 'gy'), may hold values from 0.2 to 5
- albedo: float32 [16, 128, 128], P('gx', 'gy'), may hold values from 0.1 to 0.7
- tile_faces: int32 [16, 128], P('gx', 'gy'), may hold values from 32 to 128
- face_cell: int32 [16, 128, 128], P('gx', 'gy'), may hold values from 0 to 393215, as said below
- src_tile: int32 [16, 512], P('gx', 'gy'), may hold values from 0 to 15
- dst_tile: int32 [16, 512], P('gx', 'gy'), may hold values from 0 to 127, as said below
- view_factor: float32 [16, 512, 128, 128], P('gx', 'gy'), may hold values from 0 to 0.06
- pair_count: int32 [16, 8], P('gx', 'gy'), may hold values from 16 to 64
- plane_index: int32 [16], P('gx'), may hold values from 0 to 47
Outputs:
- fields_out: float32 [5, 768, 512, 128], P(None, 'gx', 'gy')
- radiosity: float32 [16, 128, 4, 128], P('gx', 'gy')
Inputs may be any that keep to these rules, and one draw needn't show every extreme that they name: `dst_tile`: of one device's live pairs at most 8 target tiles of one device of the gy axis, and in every draw some device has all 64 pairs live and 8 of them to each device. `face_cell`: faces heat cells in the lowest quarter of the levels.
All inputs are finite; a program needn't handle non-finite values.
Results may differ from a plain program's by a relative error of at most 0.00018.
Values sent between devices are 32-bit elements; how exact they have to be, the bound alone decides.
No kernel may reach another device: no remote copies, remote signals or barrier semaphores. Data moves between devices by JAX's collectives and lax.ppermute only.
A program may use at most 128 MiB of HBM per device.

v0:
```python
import functools

import jax
import jax.numpy as jnp
from jax import lax
from jax.experimental import pallas as pl
from jax.experimental.pallas import tpu as pltpu
from jax.sharding import PartitionSpec as P

STEPS = 4
TILES_DEV = 16
HALO = STEPS
CHUNK = 8


def shifted(value, axis, steps, wrap=False):
    count = lax.axis_size(axis)
    pairs = [(i, (i + steps) % count) for i in range(count) if wrap or 0 <= i + steps < count]
    return lax.ppermute(value, axis, pairs)


def stencil_kernel(
    fields, yside, xlow, xhigh, plane, heat, hside, hlow, hhigh, out, a, b, rec, src, in_sems, out_sems, *, width, rows
):
    fields_n = fields.shape[0]
    tiles = rows // 8 + 1
    chunks = width // CHUNK
    total = width + 2 * HALO
    gx = lax.axis_index("gx")
    gy = lax.axis_index("gy")
    last_gx = lax.axis_size("gx") - 1
    last_gy = lax.axis_size("gy") - 1

    def own_copy(k):
        return pltpu.make_async_copy(
            fields.at[:, pl.ds(k * CHUNK, CHUNK)],
            a.at[:, pl.ds(HALO + k * CHUNK, CHUNK), pl.ds(0, rows)],
            in_sems.at[0, k],
        )

    def side_copy(k):
        return pltpu.make_async_copy(
            yside.at[:, pl.ds(k * CHUNK, CHUNK)],
            a.at[:, pl.ds(HALO + k * CHUNK, CHUNK), pl.ds(rows, 8)],
            in_sems.at[1, k],
        )

    def out_copy(k):
        return pltpu.make_async_copy(
            a.at[:, pl.ds(HALO + k * CHUNK, CHUNK), pl.ds(0, rows)],
            out.at[:, pl.ds(k * CHUNK, CHUNK)],
            out_sems.at[k],
        )

    low_copy = pltpu.make_async_copy(
        xlow.at[:, pl.ds(0, HALO)], a.at[:, pl.ds(0, HALO)], in_sems.at[2, 0]
    )
    high_copy = pltpu.make_async_copy(
        xhigh.at[:, pl.ds(0, HALO)], a.at[:, pl.ds(HALO + width, HALO)], in_sems.at[2, 1]
    )
    plane_copies = [
        pltpu.make_async_copy(xlow.at[:, HALO], rec.at[0], in_sems.at[2, 2]),
        pltpu.make_async_copy(plane, rec.at[1], in_sems.at[2, 3]),
        pltpu.make_async_copy(xhigh.at[:, HALO], rec.at[2], in_sems.at[2, 4]),
    ]
    block = pl.ds(HALO, width)
    heat_copies = [
        pltpu.make_async_copy(heat, src.at[block, pl.ds(0, rows)], in_sems.at[3, 0]),
        pltpu.make_async_copy(hside, src.at[block, pl.ds(rows, 8)], in_sems.at[3, 1]),
        pltpu.make_async_copy(hlow, src.at[pl.ds(0, HALO)], in_sems.at[3, 2]),
        pltpu.make_async_copy(hhigh, src.at[pl.ds(HALO + width, HALO)], in_sems.at[3, 3]),
    ]
    for copy in plane_copies:
        copy.start()
    low_copy.start()
    for copy in heat_copies:
        copy.start()
    for k in range(chunks):
        own_copy(k).start()
        side_copy(k).start()
    high_copy.start()

    zero = jnp.zeros((8, a.shape[-1]), jnp.float32)
    for f in range(fields_n):
        for j in range(tiles):
            b[f, HALO - 1, pl.ds(8 * j, 8)] = zero
            b[f, HALO + width, pl.ds(8 * j, 8)] = zero
    for copy in plane_copies:
        copy.wait()
    for s in range(3):
        for f in range(fields_n):
            for j in range(tiles):
                rec[s, f, pl.ds(8 * j, 8)] = 0.05 * rec[s, f, pl.ds(8 * j, 8)]
    low_copy.wait()
    for copy in heat_copies:
        copy.wait()

    row = lax.broadcasted_iota(jnp.int32, zero.shape, 0)
    lane = lax.broadcasted_iota(jnp.int32, zero.shape, 1)
    depth = zero.shape[1]
    first_row = row == 0
    final_row = row == 7
    up = jnp.where(lane == depth - 1, 0.0, 1.0).astype(jnp.float32)
    down = jnp.where(lane == 0, 0.0, 1.0).astype(jnp.float32)
    after = (row < 4) & (gy < last_gy)
    before = (row >= 4) & (gy > 0)
    side_mask = jnp.where(after | before, 1.0, 0.0).astype(jnp.float32)

    def plane_step(old, new, x, slot):
        for j in range(tiles):
            here = pl.ds(8 * j, 8)

            def next_rows(f):
                if j < tiles - 1:
                    return old[f, x, pl.ds(8 * j + 1, 8)]
                return jnp.where(
                    final_row,
                    pltpu.roll(old[f, x, pl.ds(0, 8)], 7, 0),
                    pltpu.roll(old[f, x, here], 7, 0),
                )

            def previous_rows(f):
                if j > 0:
                    return old[f, x, pl.ds(8 * j - 1, 8)]
                return jnp.where(
                    first_row,
                    pltpu.roll(old[f, x, pl.ds(rows, 8)], 1, 0),
                    pltpu.roll(old[f, x, here], 1, 0),
                )

            u = 0.05 * old[2, x, here]
            v = 0.05 * old[3, x, here]
            w = 0.05 * old[4, x, here]
            c_xp, c_xm = 0.02 - u, 0.02 + u
            c_yp, c_ym = 0.02 - v, 0.02 + v
            c_zp, c_zm = up * (0.02 - w), down * (0.02 + w)
            for f in range(fields_n):
                c = old[f, x, here]
                t1 = 0.83 * c + rec[slot, f, here]
                t2 = c_xp * old[f, x + 1, here] + c_xm * old[f, x - 1, here]
                t3 = c_yp * next_rows(f) + c_ym * previous_rows(f)
                t4 = c_zp * pltpu.roll(c, depth - 1, 1) + c_zm * pltpu.roll(c, 1, 1)
                fresh = (t1 + t2) + (t3 + t4)
                if f == 0:
                    fresh = fresh + src[x, here]
                if j == tiles - 1:
                    fresh = fresh * side_mask
                new[f, x, here] = fresh

    for step in range(1, STEPS + 1):
        old, new = (a, b) if step % 2 == 1 else (b, a)
        first = jnp.where(gx == 0, HALO, step)
        end = jnp.where(gx == last_gx, HALO + width, total - step)

        def body(x, carry, old=old, new=new):
            slot = jnp.where(x < HALO, 0, jnp.where(x < HALO + width, 1, 2))
            plane_step(old, new, x, slot)
            return carry

        if step == 1:
            own_copy(0).wait()
            side_copy(0).wait()

            def body1(x, carry):
                ahead = x + 1 - HALO

                @pl.when((ahead > 0) & (ahead < width) & (lax.rem(ahead, CHUNK) == 0))
                def _():
                    k = lax.div(ahead, CHUNK)
                    own_copy(k).wait()
                    side_copy(k).wait()

                @pl.when(ahead == width)
                def _():
                    high_copy.wait()

                slot = jnp.where(x < HALO, 0, jnp.where(x < HALO + width, 1, 2))
                plane_step(a, b, x, slot)
                return carry

            lax.fori_loop(first, end, body1, 0)
        elif step < STEPS:
            lax.fori_loop(first, end, body, 0)
        else:

            def last_body(x, carry, old=old, new=new):
                plane_step(old, new, x, 1)
                done = x + 1 - HALO

                @pl.when(lax.rem(done, CHUNK) == 0)
                def _():
                    out_copy(lax.div(done, CHUNK) - 1).start()

                return carry

            lax.fori_loop(HALO, HALO + width, last_body, 0)
    for k in range(chunks):
        out_copy(k).wait()


def stencil(fields, yside, xlow, xhigh, plane, heat, hside, hlow, hhigh):
    count, width, rows, depth = fields.shape
    total = width + 2 * HALO
    buffer = pltpu.VMEM((count, total, rows + 8, depth), jnp.float32)
    return pl.pallas_call(
        functools.partial(stencil_kernel, width=width, rows=rows),
        out_shape=jax.ShapeDtypeStruct(fields.shape, jnp.float32),
        in_specs=[pl.BlockSpec(memory_space=pl.ANY)] * 9,
        out_specs=pl.BlockSpec(memory_space=pl.ANY),
        scratch_shapes=[
            buffer,
            buffer,
            pltpu.VMEM((3, count, rows + 8, depth), jnp.float32),
            pltpu.VMEM((total, rows + 8, depth), jnp.float32),
            pltpu.SemaphoreType.DMA((4, max(width // CHUNK, 5))),
            pltpu.SemaphoreType.DMA((width // CHUNK,)),
        ],
        compiler_params=pltpu.CompilerParams(vmem_limit_bytes=48 * 1024 * 1024),
        cost_estimate=pl.CostEstimate(flops=160_000_000, bytes_accessed=20_000_000, transcendentals=0),
        name="stencil",
    )(fields, yside, xlow, xhigh, plane, heat, hside, hlow, hhigh)


NT = (((1,), (1,)), ((), ()))
PAIR_CHUNK = 8


def split(value):
    high = value.astype(jnp.bfloat16)
    return high, (value - high.astype(jnp.float32)).astype(jnp.bfloat16)


def live_faces(tile_faces, t, shape):
    lane = lax.broadcasted_iota(jnp.int32, shape, 1)
    return jnp.where(lane < tile_faces[0, t], 1.0, 0.0).astype(jnp.float32)


def summed(arrived, t, tiles):
    total = arrived[t]
    for g in range(1, arrived.shape[0] // tiles):
        total = total + arrived[g * tiles + t]
    return total


def flux_kernel(tile_faces, sources, targets, count, emission, albedo, arrived, factors, out, held, lhs, sems):
    tiles, bands, faces = emission.shape
    pairs = factors.shape[0]
    chunks = pairs // PAIR_CHUNK

    def chunk_copy(k):
        part = pl.ds(k * PAIR_CHUNK, PAIR_CHUNK)
        return pltpu.make_async_copy(factors.at[part], held.at[part], sems.at[k])

    for k in range(chunks):
        chunk_copy(k).start()
    out[...] = jnp.zeros_like(out)
    for t in range(tiles):
        radiosity = emission[t]
        if arrived is not None:
            radiosity = radiosity + albedo[pl.ds(t, 1), :] * summed(arrived, t, tiles)
        radiosity = live_faces(tile_faces, t, (bands, faces)) * radiosity
        high, low = split(radiosity)
        high, low = high.astype(jnp.float32), low.astype(jnp.float32)
        nothing = jnp.zeros_like(high)
        left = jnp.concatenate([high, low, nothing, nothing], axis=0)
        right = jnp.concatenate([high, nothing, nothing, nothing], axis=0)
        lhs[t] = jnp.concatenate([left, right], axis=1).astype(jnp.bfloat16)

    def chunk_step(k, carry):
        chunk_copy(k).wait()
        for i in range(PAIR_CHUNK // 2):
            first = k * PAIR_CHUNK + 2 * i
            both = held[pl.ds(first, 2)].reshape(2 * faces, faces)
            rhs = jnp.concatenate(split(both), axis=1)
            rows = jnp.concatenate([lhs[sources[0, first]], lhs[sources[0, first + 1]]], axis=0)
            got = lax.dot_general(rows, rhs, NT, preferred_element_type=jnp.float32)
            for n in range(2):
                part = got[16 * n : 16 * n + 8, n * faces : (n + 1) * faces]
                flux = part[:bands] + part[bands : 2 * bands]
                target = targets[0, first + n]
                out[target] = out[target] + jnp.where(first + n < count[0, 0], flux, 0.0)
        return carry

    lax.fori_loop(0, chunks, chunk_step, 0)


def flux(tile_faces, sources, targets, count, emission, albedo, arrived, factors, slab_tiles):
    tiles, bands, faces = emission.shape
    pairs = factors.shape[0]
    scalar = pl.BlockSpec(memory_space=pltpu.SMEM)
    vector = pl.BlockSpec(memory_space=pltpu.VMEM)
    given = [tile_faces, sources, targets, count, emission, albedo, factors]
    specs = [scalar] * 4 + [vector] * 2 + [pl.BlockSpec(memory_space=pl.ANY)]
    if arrived is None:
        def kernel(a, b, c, d, e, f, factors_, *rest):
            flux_kernel(a, b, c, d, e, f, None, factors_, *rest)
    else:
        given.append(arrived)
        specs.append(vector)

        def kernel(a, b, c, d, e, f, factors_, arrived_, *rest):
            flux_kernel(a, b, c, d, e, f, arrived_, factors_, *rest)

    return pl.pallas_call(
        kernel,
        out_shape=jax.ShapeDtypeStruct((slab_tiles, bands, faces), jnp.float32),
        in_specs=specs,
        out_specs=vector,
        scratch_shapes=[
            pltpu.VMEM(factors.shape, jnp.float32),
            pltpu.VMEM((tiles, 16, 2 * faces), jnp.bfloat16),
            pltpu.SemaphoreType.DMA((pairs // PAIR_CHUNK,)),
        ],
        compiler_params=pltpu.CompilerParams(vmem_limit_bytes=16 * 1024 * 1024),
        cost_estimate=pl.CostEstimate(flops=12_000_000, bytes_accessed=12_000_000, transcendentals=0),
        name="flux",
    )(*given)


def heat_kernel(tile_faces, emission, albedo, cells, arrived, radiosity, heat, low, high, *, width, rows, depth):
    tiles, bands, faces = emission.shape
    quarter = depth // 4
    near = rows // 4
    picks, weights = [], []
    for t in range(tiles):
        live = live_faces(tile_faces, t, (bands, faces))
        incoming = summed(arrived, t, tiles)
        row = albedo[pl.ds(t, 1), :]
        radiosity[t] = live * (emission[t] + row * incoming)
        absorbed = 0.1 * live[:1] * (1.0 - row) * jnp.sum(incoming, axis=0, keepdims=True)
        cell = cells[pl.ds(t, 1), :]
        level = cell & (depth - 1)
        y = (cell >> (depth.bit_length() - 1)) & (rows - 1)
        x = cell >> (depth.bit_length() + rows.bit_length() - 2)
        pick_of = x * near + (y & (near - 1))
        column_of = (y // near) * quarter + level
        at_row = lax.broadcasted_iota(jnp.int32, (width * near, faces), 0) == pick_of
        picks.append(jnp.where(at_row, 1.0, 0.0).astype(jnp.bfloat16))
        at_column = lax.broadcasted_iota(jnp.int32, (4 * quarter, faces), 0) == column_of
        top = absorbed.astype(jnp.bfloat16).astype(jnp.float32)
        weights.append(
            jnp.concatenate(
                [jnp.where(at_column, top, 0.0), jnp.where(at_column, absorbed - top, 0.0)], axis=0
            ).astype(jnp.bfloat16)
        )
    picks = jnp.concatenate(picks, axis=1)
    weights = jnp.concatenate(weights, axis=1)
    got = lax.dot_general(picks, weights, NT, preferred_element_type=jnp.float32)
    got = got[:, :depth] + got[:, depth:]
    lane = lax.broadcasted_iota(jnp.int32, (8, depth), 1)
    for x in range(width):
        for q in range(4):
            for half in range(near // 8):
                block = got[x * near + 8 * half : x * near + 8 * half + 8]
                if q:
                    block = pltpu.roll(block, depth - q * quarter, 1)
                block = jnp.where(lane < quarter, block, 0.0)
                heat[x, pl.ds(q * near + 8 * half, 8)] = block
                if q == 0 and half == 0:
                    low[x] = block[:HALO]
                if q == 3 and half == near // 8 - 1:
                    high[x] = block[8 - HALO :]


def heating(tile_faces, emission, albedo, cells, arrived, width, rows, depth):
    scalar = pl.BlockSpec(memory_space=pltpu.SMEM)
    vector = pl.BlockSpec(memory_space=pltpu.VMEM)
    side = jax.ShapeDtypeStruct((width, HALO, depth), jnp.float32)
    return pl.pallas_call(
        functools.partial(heat_kernel, width=width, rows=rows, depth=depth),
        out_shape=(
            jax.ShapeDtypeStruct(emission.shape, jnp.float32),
            jax.ShapeDtypeStruct((width, rows, depth), jnp.float32),
            side,
            side,
        ),
        in_specs=[scalar] + [vector] * 4,
        out_specs=(vector,) * 4,
        compiler_params=pltpu.CompilerParams(vmem_limit_bytes=24 * 1024 * 1024),
        cost_estimate=pl.CostEstimate(flops=12_000_000, bytes_accessed=4_000_000, transcendentals=0),
        name="heating",
    )(tile_faces, emission, albedo, cells, arrived)


def with_sides(cells):
    rows = cells.shape[-2]
    after = shifted(cells[..., :HALO, :], "gy", -1)
    before = shifted(cells[..., rows - HALO :, :], "gy", 1)
    return jnp.concatenate([after, before], axis=-2)


def local(
    fields,
    emission,
    albedo,
    tile_faces,
    face_cell,
    src_tile,
    dst_tile,
    view_factor,
    pair_count,
    plane_index,
):
    width = fields.shape[1]
    rows = fields.shape[2]
    depth = fields.shape[3]
    n_gx = lax.axis_size("gx")
    n_gy = lax.axis_size("gy")

    yside = with_sides(fields)
    own = emission[0], albedo[0]
    pairs = src_tile, dst_tile, pair_count
    slab_tiles = n_gy * TILES_DEV
    outgoing = flux(tile_faces, *pairs, *own, None, view_factor[0], slab_tiles)
    arrived = lax.all_to_all(outgoing, "gy", split_axis=0, concat_axis=0, tiled=True)

    plane = jnp.concatenate(
        [
            lax.dynamic_index_in_dim(fields, plane_index[0], 1, keepdims=False),
            lax.dynamic_index_in_dim(yside, plane_index[0], 1, keepdims=False),
        ],
        axis=1,
    )
    plane = shifted(plane, "gx", n_gx // 2, wrap=True)

    def slab(start):
        part = slice(start, start + HALO)
        cells = jnp.concatenate([fields[:, part], yside[:, part]], axis=2)
        return jnp.concatenate([cells, plane[:, None]], axis=1)

    xlow = shifted(slab(width - HALO), "gx", 1)
    xhigh = shifted(slab(0), "gx", -1)

    outgoing = flux(tile_faces, *pairs, *own, arrived, view_factor[0], slab_tiles)
    arrived = lax.all_to_all(outgoing, "gy", split_axis=0, concat_axis=0, tiled=True)
    radiosity, heat, low, high = heating(tile_faces, *own, face_cell[0], arrived, width, rows, depth)
    hside = jnp.concatenate([shifted(low, "gy", -1), shifted(high, "gy", 1)], axis=1)
    hends = [jnp.concatenate([heat[p], hside[p]], axis=1) for p in (slice(width - HALO, width), slice(0, HALO))]
    hlow = shifted(hends[0], "gx", 1)
    hhigh = shifted(hends[1], "gx", -1)
    stepped = stencil(fields, yside, xlow, xhigh, plane, heat, hside, hlow, hhigh)
    return (stepped, radiosity[None])


def solution(mesh):
    return jax.shard_map(
        local,
        mesh=mesh,
        in_specs=(
            P(None, "gx", "gy", None),
            P("gx", "gy", None, None),
            P("gx", "gy", None),
            P("gx", "gy"),
            P("gx", "gy", None),
            P("gx", "gy"),
            P("gx", "gy"),
            P("gx", "gy", None, None),
            P("gx", "gy"),
            P("gx"),
        ),
        out_specs=(P(None, "gx", "gy", None), P("gx", "gy", None, None)),
        check_vma=False,
    )
```

profile of v0, /device:TPU:40, one launch (start us, length us, event | category | flops | bytes accessed | tf_op | source)
XLA Modules:
  0.0 115.8 jit_solution(15527438703994899321)
XLA Ops:
  0.7 1.7 %fusion.7 = (f32[5,48,4,128]{3,2,1,0:T(4,128)S(1)}, f32[5,48,4,128]{3,2,1,0:T(4,128)S(1)}) fusion(f32[5,48,64,128]{3,2,1,0:T(8,128)} %fields.1), kind=kLoop, calls=%fused_computation.25 | loop fusion | bytes 1966080 | tf_op jit(solution)/shard_map/slice | solution.py:387
  2.4 1.9 %collective-permute-start = (f32[5,48,4,128]{3,2,1,0:T(4,128)S(1)}, f32[5,48,4,128]{3,2,1,0:T(4,128)S(1)}, u32[]{:S(2)}, u32[]{:S(2)}) collective-permute-start(f32[5,48,4,128]{3,2,1,0:T(4,128)S(1)} %get-tuple-element.12), channel_id=1, source_target_pairs={{1,0},{2,1},{3,2},{4,3},{5,4},{6,5},{7,6},{9,8},{10,9},{11,10},{12... | collective-permute-start | bytes 1474568 | tf_op jit(solution)/shard_map/ppermute | solution.py:19
  4.3 2.4 %collective-permute-start.1 = (f32[5,48,4,128]{3,2,1,0:T(4,128)S(1)}, f32[5,48,4,128]{3,2,1,0:T(4,128)S(1)}, u32[]{:S(2)}, u32[]{:S(2)}) collective-permute-start(f32[5,48,4,128]{3,2,1,0:T(4,128)S(1)} %get-tuple-element.13), channel_id=1, source_target_pairs={{0,1},{1,2},{2,3},{3,4},{4,5},{5,6},{6,7},{8,9},{9,10},{10,11},{11... | collective-permute-start | bytes 1474568 | tf_op jit(solution)/shard_map/ppermute | solution.py:19
  7.4 2.2 %copy-done = f32[1,64,128,128]{3,2,1,0:T(8,128)S(1)} copy-done((f32[1,64,128,128]{3,2,1,0:T(8,128)S(1)}, f32[1,64,128,128]{3,2,1,0:T(8,128)}, u32[]{:S(2)}) %copy-start) | copy-done | bytes 4194328
  9.6 0.8 copy-done.2
  13.0 3.9 %flux.2 = f32[128,4,128]{2,1,0:T(4,128)} custom-call(s32[1,16]{1,0:T(1,128)S(1)} %copy-done.7, s32[1,64]{1,0:T(1,128)S(1)} %copy-done.9, s32[1,64]{1,0:T(1,128)S(1)} %copy-done.11, s32[1,1]{1,0:T(1,128)S(6)} %copy.14.d, f32[16,4,128]{2,1,0:T(4,128)S(1)} %bitcast.19, f32[16,128]{1,0:T(8,128)S(1)} %bitcast.22, f32[64,128,128]{2,1,0:T(8,128)S(1)} %bitcast.16), custom_call_target="tpu_custom_call" | custom-call | flops 12000000 | bytes 12000000 | tf_op jit(solution)/shard_map/flux/pallas_call | solution.py:304
  16.9 5.6 %all-to-all-start = ((f32[128,4,128]{2,1,0:T(4,128)}), f32[128,4,128]{2,1,0:T(4,128)S(1)}, u32[]{:S(2)}, u32[]{:S(2)}) async-start(f32[128,4,128]{2,1,0:T(4,128)} %flux.2), calls=%async_computation | async-start | bytes 524288 | tf_op jit(solution)/shard_map/all_to_all | solution.py:415
  23.2 0.9 dynamic-slice_bitcast_fusion
  24.2 3.1 %collective-permute-start.2 = (f32[5,72,128]{2,1,0:T(8,128)S(1)}, f32[5,72,128]{2,1,0:T(8,128)S(1)}, u32[]{:S(2)}, u32[]{:S(2)}) collective-permute-start(f32[5,72,128]{2,1,0:T(8,128)S(1)} %pad_maximum_fusion.4), channel_id=1, source_target_pairs={{0,64},{8,72},{16,80},{24,88},{32,96},{40,104},{48,112},{56,120},{... | collective-permute-start | bytes 552968 | tf_op jit(solution)/shard_map/ppermute | solution.py:19
  27.2 1.4 %fusion.6 = (f32[5,4,64,128]{3,2,1,0:T(8,128)S(1)}, f32[5,4,64,128]{3,2,1,0:T(8,128)S(1)}) fusion(f32[5,48,64,128]{3,2,1,0:T(8,128)} %fields.1), kind=kLoop, calls=%fused_computation.24 | loop fusion | bytes 2621440 | tf_op jit(solution)/shard_map/slice | solution.py:428
  28.7 2.2 %copy-done.1 = f32[1,64,128,128]{3,2,1,0:T(8,128)S(1)} copy-done((f32[1,64,128,128]{3,2,1,0:T(8,128)S(1)}, f32[1,64,128,128]{3,2,1,0:T(8,128)}, u32[]{:S(2)}) %copy-start.1) | copy-done | bytes 4194328
  30.9 3.9 %flux.3 = f32[128,4,128]{2,1,0:T(4,128)} custom-call(s32[1,16]{1,0:T(1,128)S(1)} %copy-done.8, s32[1,64]{1,0:T(1,128)S(1)} %copy-done.10, s32[1,64]{1,0:T(1,128)S(1)} %copy-done.12, s32[1,1]{1,0:T(1,128)S(6)} %copy.14.d, f32[16,4,128]{2,1,0:T(4,128)S(1)} %bitcast.20, f32[16,128]{1,0:T(8,128)S(1)} %bitcast.23, f32[64,128,128]{2,1,0:T(8,128)S(1)} %bitcast.17, ...), custom_call_target="tpu_custom_call" | custom-call | flops 12000000 | bytes 12000000 | tf_op jit(solution)/shard_map/flux/pallas_call | solution.py:304
  34.8 4.8 %all-to-all-start.1 = ((f32[128,4,128]{2,1,0:T(4,128)}), f32[128,4,128]{2,1,0:T(4,128)S(1)}, u32[]{:S(2)}, u32[]{:S(2)}) async-start(f32[128,4,128]{2,1,0:T(4,128)} %flux.3), calls=%async_computation.1 | async-start | bytes 524288 | tf_op jit(solution)/shard_map/all_to_all | solution.py:435
  39.7 1.4 %pad_maximum_fusion.1 = (f32[5,5,72,128]{3,2,1,0:T(8,128)}, f32[5,5,72,128]{3,2,1,0:T(8,128)}) fusion(f32[5,1,72,128]{3,2,1,0:T(8,128)S(1)} %bitcast.18, f32[5,4,8,128]{3,2,1,0:T(8,128)S(1)} %get-tuple-element.16, f32[5,4,64,128]{3,2,1,0:T(8,128)S(1)} %get-tuple-element.10, f32[5,4,8,128]{3,2,1,0:T(8,128)S(1)} %get-tuple-element.17, ...), kind=kLoop, calls=%fused_computation.7 | loop fusion | flops 921600 | bytes 3502080 | tf_op jit(solution)/shard_map/concatenate | solution.py:429
  41.1 5.1 %collective-permute-start.4 = (f32[5,5,72,128]{3,2,1,0:T(8,128)}, f32[5,5,72,128]{3,2,1,0:T(8,128)S(1)}, u32[]{:S(2)}, u32[]{:S(2)}) collective-permute-start(f32[5,5,72,128]{3,2,1,0:T(8,128)} %get-tuple-element.20), channel_id=1, source_target_pairs={{8,0},{16,8},{24,16},{32,24},{40,32},{48,40},{56,48},{64,56},{72,6... | collective-permute-start | bytes 2764808 | tf_op jit(solution)/shard_map/ppermute | solution.py:19
  46.2 1.9 %collective-permute-start.3 = (f32[5,5,72,128]{3,2,1,0:T(8,128)}, f32[5,5,72,128]{3,2,1,0:T(8,128)S(1)}, u32[]{:S(2)}, u32[]{:S(2)}) collective-permute-start(f32[5,5,72,128]{3,2,1,0:T(8,128)} %get-tuple-element.21), channel_id=1, source_target_pairs={{0,8},{8,16},{16,24},{24,32},{32,40},{40,48},{48,56},{56,64},{64,7... | collective-permute-start | bytes 2764808 | tf_op jit(solution)/shard_map/ppermute | solution.py:19
  48.1 2.4 %heating.1 = (f32[16,4,128]{2,1,0:T(4,128)}, f32[48,64,128]{2,1,0:T(8,128)S(1)}, f32[48,4,128]{2,1,0:T(4,128)S(1)}, f32[48,4,128]{2,1,0:T(4,128)S(1)}) custom-call(s32[1,16]{1,0:T(1,128)S(1)} %copy-done.8, f32[16,4,128]{2,1,0:T(4,128)S(1)} %bitcast.21, f32[16,128]{1,0:T(8,128)S(1)} %bitcast.24, s32[16,128]{1,0:T(8,128)S(1)} %bitcast.25, ...), custom_call_target="tpu_custom_call" | custom-call | flops 12000000 | bytes 4000000 | tf_op jit(solution)/shard_map/heating/pallas_call | solution.py:369
  50.5 1.9 %collective-permute-start.5 = (f32[48,4,128]{2,1,0:T(4,128)S(1)}, f32[48,4,128]{2,1,0:T(4,128)S(1)}, u32[]{:S(2)}, u32[]{:S(2)}) collective-permute-start(f32[48,4,128]{2,1,0:T(4,128)S(1)} %get-tuple-element.7), channel_id=1, source_target_pairs={{1,0},{2,1},{3,2},{4,3},{5,4},{6,5},{7,6},{9,8},{10,9},{11,10},{12... | collective-permute-start | bytes 294920 | tf_op jit(solution)/shard_map/ppermute | solution.py:19
  52.4 2.4 %collective-permute-start.6 = (f32[48,4,128]{2,1,0:T(4,128)S(1)}, f32[48,4,128]{2,1,0:T(4,128)S(1)}, u32[]{:S(2)}, u32[]{:S(2)}) collective-permute-start(f32[48,4,128]{2,1,0:T(4,128)S(1)} %get-tuple-element.8), channel_id=1, source_target_pairs={{0,1},{1,2},{2,3},{3,4},{4,5},{5,6},{6,7},{8,9},{9,10},{10,11},{11... | collective-permute-start | bytes 294920 | tf_op jit(solution)/shard_map/ppermute | solution.py:19
  54.9 3.5 %collective-permute-done.6 = f32[48,4,128]{2,1,0:T(4,128)S(1)} collective-permute-done((f32[48,4,128]{2,1,0:T(4,128)S(1)}, f32[48,4,128]{2,1,0:T(4,128)S(1)}, u32[]{:S(2)}, u32[]{:S(2)}) %collective-permute-start.6) | collective-permute-done | bytes 98336 | tf_op jit(solution)/shard_map/ppermute | solution.py:19
  58.4 2.2 %collective-permute-start.7 = (f32[4,72,128]{2,1,0:T(8,128)S(1)}, f32[4,72,128]{2,1,0:T(8,128)S(1)}, u32[]{:S(2)}, u32[]{:S(2)}) collective-permute-start(f32[4,72,128]{2,1,0:T(8,128)S(1)} %pad_maximum_fusion.5), channel_id=1, source_target_pairs={{0,8},{8,16},{16,24},{24,32},{32,40},{40,48},{48,56},{56,64},{64,7... | collective-permute-start | bytes 442376 | tf_op jit(solution)/shard_map/ppermute | solution.py:19
  60.6 5.7 %collective-permute-start.8 = (f32[4,72,128]{2,1,0:T(8,128)S(1)}, f32[4,72,128]{2,1,0:T(8,128)S(1)}, u32[]{:S(2)}, u32[]{:S(2)}) collective-permute-start(f32[4,72,128]{2,1,0:T(8,128)S(1)} %pad_maximum_fusion.6), channel_id=1, source_target_pairs={{8,0},{16,8},{24,16},{32,24},{40,32},{48,40},{56,48},{64,56},{72,6... | collective-permute-start | bytes 442376 | tf_op jit(solution)/shard_map/ppermute | solution.py:19
  66.6 9.1 %collective-permute-done.7.hlow = f32[4,72,128]{2,1,0:T(8,128)S(1)} collective-permute-done((f32[4,72,128]{2,1,0:T(8,128)S(1)}, f32[4,72,128]{2,1,0:T(8,128)S(1)}, u32[]{:S(2)}, u32[]{:S(2)}) %collective-permute-start.7) | collective-permute-done | bytes 147488 | tf_op jit(solution)/shard_map/ppermute | solution.py:19
  75.8 40.0 %stencil.1 = f32[5,48,64,128]{3,2,1,0:T(8,128)} custom-call(f32[5,48,64,128]{3,2,1,0:T(8,128)} %fields.1, f32[5,48,8,128]{3,2,1,0:T(8,128)S(1)} %pad_maximum_fusion.yside, f32[5,5,72,128]{3,2,1,0:T(8,128)S(1)} %collective-permute-done.3.xlow, f32[5,5,72,128]{3,2,1,0:T(8,128)S(1)} %collective-permute-done.4.xhigh, ...), custom_call_target="tpu_custom_call" | custom-call | flops 160000000 | bytes 20000000 | tf_op jit(solution)/shard_map/stencil/pallas_call | solution.py:205
  (41 shorter events, 3.1 us)
Async XLA Ops:
  0.6 28.1 %copy-start.8 = (s32[1,16]{1,0:T(1,128)S(1)}, s32[1,16]{1,0:T(1,128)}, u32[]{:S(2)}) copy-start(s32[1,16]{1,0:T(1,128)} %tile_faces.1) | copy-start | bytes 196
  0.6 28.1 %copy-start.12 = (s32[1,64]{1,0:T(1,128)S(1)}, s32[1,64]{1,0:T(1,128)}, u32[]{:S(2)}) copy-start(s32[1,64]{1,0:T(1,128)} %c.3) | copy-start | bytes 772
  0.7 28.0 %copy-start.10 = (s32[1,64]{1,0:T(1,128)S(1)}, s32[1,64]{1,0:T(1,128)}, u32[]{:S(2)}) copy-start(s32[1,64]{1,0:T(1,128)} %b.3) | copy-start | bytes 772
  0.7 28.0 %copy-start.5 = (f32[1,16,128]{2,1,0:T(8,128)S(1)}, f32[1,16,128]{2,1,0:T(8,128)}, u32[]{:S(2)}) copy-start(f32[1,16,128]{2,1,0:T(8,128)} %param.12) | copy-start | bytes 24580
  0.7 28.0 %copy-start.3 = (f32[1,16,4,128]{3,2,1,0:T(4,128)S(1)}, f32[1,16,4,128]{3,2,1,0:T(4,128)}, u32[]{:S(2)}) copy-start(f32[1,16,4,128]{3,2,1,0:T(4,128)} %param.11) | copy-start | bytes 98308
  2.4 21.7 %collective-permute-start = (f32[5,48,4,128]{3,2,1,0:T(4,128)S(1)}, f32[5,48,4,128]{3,2,1,0:T(4,128)S(1)}, u32[]{:S(2)}, u32[]{:S(2)}) collective-permute-start(f32[5,48,4,128]{3,2,1,0:T(4,128)S(1)} %get-tuple-element.12), channel_id=1, source_target_pairs={{1,0},{2,1},{3,2},{4,3},{5,4},{6,5},{7,6},{9,8},{10,9},{11,10},{12... | collective-permute-start | bytes 1474568 | tf_op jit(solution)/shard_map/ppermute | solution.py:19
  4.3 19.8 %collective-permute-start.1 = (f32[5,48,4,128]{3,2,1,0:T(4,128)S(1)}, f32[5,48,4,128]{3,2,1,0:T(4,128)S(1)}, u32[]{:S(2)}, u32[]{:S(2)}) collective-permute-start(f32[5,48,4,128]{3,2,1,0:T(4,128)S(1)} %get-tuple-element.13), channel_id=1, source_target_pairs={{0,1},{1,2},{2,3},{3,4},{4,5},{5,6},{6,7},{8,9},{9,10},{10,11},{11... | collective-permute-start | bytes 1474568 | tf_op jit(solution)/shard_map/ppermute | solution.py:19
  7.4 2.2 %copy-start = (f32[1,64,128,128]{3,2,1,0:T(8,128)S(1)}, f32[1,64,128,128]{3,2,1,0:T(8,128)}, u32[]{:S(2)}) copy-start(f32[1,64,128,128]{3,2,1,0:T(8,128)} %param.17) | copy-start | bytes 12582916
  9.6 0.8 copy-start.2
  10.3 0.7 copy-start.4
  11.0 0.7 copy-start.7
  11.7 0.7 copy-start.9
  12.3 0.7 copy-start.11
  16.9 31.2 %copy-start.6 = (s32[1,16,128]{2,1,0:T(8,128)S(1)}, s32[1,16,128]{2,1,0:T(8,128)}, u32[]{:S(2)}) copy-start(s32[1,16,128]{2,1,0:T(8,128)} %param.14) | copy-start | bytes 24580
  16.9 11.8 %all-to-all-start = ((f32[128,4,128]{2,1,0:T(4,128)}), f32[128,4,128]{2,1,0:T(4,128)S(1)}, u32[]{:S(2)}, u32[]{:S(2)}) async-start(f32[128,4,128]{2,1,0:T(4,128)} %flux.2), calls=%async_computation | async-start | bytes 524288 | tf_op jit(solution)/shard_map/all_to_all | solution.py:415
  24.2 15.5 %collective-permute-start.2 = (f32[5,72,128]{2,1,0:T(8,128)S(1)}, f32[5,72,128]{2,1,0:T(8,128)S(1)}, u32[]{:S(2)}, u32[]{:S(2)}) collective-permute-start(f32[5,72,128]{2,1,0:T(8,128)S(1)} %pad_maximum_fusion.4), channel_id=1, source_target_pairs={{0,64},{8,72},{16,80},{24,88},{32,96},{40,104},{48,112},{56,120},{... | collective-permute-start | bytes 552968 | tf_op jit(solution)/shard_map/ppermute | solution.py:19
  28.7 2.2 %copy-start.1 = (f32[1,64,128,128]{3,2,1,0:T(8,128)S(1)}, f32[1,64,128,128]{3,2,1,0:T(8,128)}, u32[]{:S(2)}) copy-start(f32[1,64,128,128]{3,2,1,0:T(8,128)} %param.17) | copy-start | bytes 12582916
  34.8 13.3 %all-to-all-start.1 = ((f32[128,4,128]{2,1,0:T(4,128)}), f32[128,4,128]{2,1,0:T(4,128)S(1)}, u32[]{:S(2)}, u32[]{:S(2)}) async-start(f32[128,4,128]{2,1,0:T(4,128)} %flux.3), calls=%async_computation.1 | async-start | bytes 524288 | tf_op jit(solution)/shard_map/all_to_all | solution.py:435
  41.1 34.7 %collective-permute-start.4 = (f32[5,5,72,128]{3,2,1,0:T(8,128)}, f32[5,5,72,128]{3,2,1,0:T(8,128)S(1)}, u32[]{:S(2)}, u32[]{:S(2)}) collective-permute-start(f32[5,5,72,128]{3,2,1,0:T(8,128)} %get-tuple-element.20), channel_id=1, source_target_pairs={{8,0},{16,8},{24,16},{32,24},{40,32},{48,40},{56,48},{64,56},{72,6... | collective-permute-start | bytes 2764808 | tf_op jit(solution)/shard_map/ppermute | solution.py:19
  46.2 29.6 %collective-permute-start.3 = (f32[5,5,72,128]{3,2,1,0:T(8,128)}, f32[5,5,72,128]{3,2,1,0:T(8,128)S(1)}, u32[]{:S(2)}, u32[]{:S(2)}) collective-permute-start(f32[5,5,72,128]{3,2,1,0:T(8,128)} %get-tuple-element.21), channel_id=1, source_target_pairs={{0,8},{8,16},{16,24},{24,32},{32,40},{40,48},{48,56},{56,64},{64,7... | collective-permute-start | bytes 2764808 | tf_op jit(solution)/shard_map/ppermute | solution.py:19
  50.5 4.4 %collective-permute-start.5 = (f32[48,4,128]{2,1,0:T(4,128)S(1)}, f32[48,4,128]{2,1,0:T(4,128)S(1)}, u32[]{:S(2)}, u32[]{:S(2)}) collective-permute-start(f32[48,4,128]{2,1,0:T(4,128)S(1)} %get-tuple-element.7), channel_id=1, source_target_pairs={{1,0},{2,1},{3,2},{4,3},{5,4},{6,5},{7,6},{9,8},{10,9},{11,10},{12... | collective-permute-start | bytes 294920 | tf_op jit(solution)/shard_map/ppermute | solution.py:19
  52.4 5.9 %collective-permute-start.6 = (f32[48,4,128]{2,1,0:T(4,128)S(1)}, f32[48,4,128]{2,1,0:T(4,128)S(1)}, u32[]{:S(2)}, u32[]{:S(2)}) collective-permute-start(f32[48,4,128]{2,1,0:T(4,128)S(1)} %get-tuple-element.8), channel_id=1, source_target_pairs={{0,1},{1,2},{2,3},{3,4},{4,5},{5,6},{6,7},{8,9},{9,10},{10,11},{11... | collective-permute-start | bytes 294920 | tf_op jit(solution)/shard_map/ppermute | solution.py:19
  58.4 17.4 %collective-permute-start.7 = (f32[4,72,128]{2,1,0:T(8,128)S(1)}, f32[4,72,128]{2,1,0:T(8,128)S(1)}, u32[]{:S(2)}, u32[]{:S(2)}) collective-permute-start(f32[4,72,128]{2,1,0:T(8,128)S(1)} %pad_maximum_fusion.5), channel_id=1, source_target_pairs={{0,8},{8,16},{16,24},{24,32},{32,40},{40,48},{48,56},{56,64},{64,7... | collective-permute-start | bytes 442376 | tf_op jit(solution)/shard_map/ppermute | solution.py:19
  60.6 15.2 %collective-permute-start.8 = (f32[4,72,128]{2,1,0:T(8,128)S(1)}, f32[4,72,128]{2,1,0:T(8,128)S(1)}, u32[]{:S(2)}, u32[]{:S(2)}) collective-permute-start(f32[4,72,128]{2,1,0:T(8,128)S(1)} %pad_maximum_fusion.6), channel_id=1, source_target_pairs={{8,0},{16,8},{24,16},{32,24},{40,32},{48,40},{56,48},{64,56},{72,6... | collective-permute-start | bytes 442376 | tf_op jit(solution)/shard_map/ppermute | solution.py:19
where the time goes:
time: 117 us; the launch traced here: 116 us
  Pallas kernels  50.2 us (43%)
  starting transfers between devices  37.1 us (32%)
  waiting for transfers between devices  12.6 us (11%)
  local copies, waits for them, and re-layouts  11.9 us (10%)
  between operations  2.26 us (2%)
  other arithmetic  1.74 us (1%)
    pallas_call x1, Pallas kernels, stencil(): pl.pallas_call(functools.partial(stencil_kernel, width=width, rows=rows),...  40 us
    ppermute x9, starting transfers between devices, shifted(): return lax.ppermute(value, axis, pairs)  26.7 us
    ppermute x9, waiting for transfers between devices, shifted(): return lax.ppermute(value, axis, pairs)  12.6 us
    all_to_all x2, starting transfers between devices, local(): lax.all_to_all(outgoing, 'gy', split_axis=0, concat_axis=0, tiled=True)  10.4 us
    unnamed x26, local copies, waits for them, and re-layouts  7.82 us
    pallas_call x2, Pallas kernels, flux(): pl.pallas_call(kernel, out_shape=jax.ShapeDtypeStruct((slab_tiles, bands,...  7.8 us
    pallas_call x1, Pallas kernels, heating(): pl.pallas_call(functools.partial(heat_kernel, width=width, rows=rows, dep...  2.36 us
  transfers between devices with their start and end apart: 11, of which 2 were waited for; matrix products, arithmetic and copies ran while one was open for 4% of the time, Pallas kernels for 9%

commit v1 on v0

v1 whole, which is shorter than its diff:
```python
import functools

import jax
import jax.numpy as jnp
from jax import lax
from jax.experimental import pallas as pl
from jax.experimental.pallas import tpu as pltpu
from jax.sharding import PartitionSpec as P

STEPS = 4
TILES_DEV = 16
HALO = STEPS
CHUNK = 8
GROUP = 4


def shifted(value, axis, steps, wrap=False):
    count = lax.axis_size(axis)
    pairs = [(i, (i + steps) % count) for i in range(count) if wrap or 0 <= i + steps < count]
    return lax.ppermute(value, axis, pairs)


def stencil_kernel(
    fields, yside, xlow, xhigh, plane, heat, ends, out, a, b, rec, packed, src, in_sems, out_sems, *, width, rows
):
    fields_n = fields.shape[0]
    tiles = rows // 8 + 1
    chunks = width // CHUNK
    total = width + 2 * HALO
    gx = lax.axis_index("gx")
    gy = lax.axis_index("gy")
    last_gx = lax.axis_size("gx") - 1
    last_gy = lax.axis_size("gy") - 1

    def own_copy(k):
        return pltpu.make_async_copy(
            fields.at[:, pl.ds(k * CHUNK, CHUNK)],
            a.at[:, pl.ds(HALO + k * CHUNK, CHUNK), pl.ds(0, rows)],
            in_sems.at[0, k],
        )

    def side_copy(k):
        return pltpu.make_async_copy(
            yside.at[:, pl.ds(k * CHUNK, CHUNK)],
            a.at[:, pl.ds(HALO + k * CHUNK, CHUNK), pl.ds(rows, 8)],
            in_sems.at[1, k],
        )

    def out_copy(k):
        return pltpu.make_async_copy(
            a.at[:, pl.ds(HALO + k * CHUNK, CHUNK), pl.ds(0, rows)],
            out.at[:, pl.ds(k * CHUNK, CHUNK)],
            out_sems.at[k],
        )

    low_copy = pltpu.make_async_copy(
        xlow, a.at[:, pl.ds(0, HALO)], in_sems.at[2, 0]
    )
    high_copy = pltpu.make_async_copy(
        xhigh, a.at[:, pl.ds(HALO + width, HALO)], in_sems.at[2, 1]
    )
    heat_rows = rows // 4 + 8
    near = HALO * heat_rows
    plane_copies = [
        pltpu.make_async_copy(ends.at[0, pl.ds(near, plane.shape[0])], rec.at[0], in_sems.at[2, 2]),
        pltpu.make_async_copy(plane, rec.at[1], in_sems.at[2, 3]),
        pltpu.make_async_copy(ends.at[1, pl.ds(near, plane.shape[0])], rec.at[2], in_sems.at[2, 4]),
    ]
    heat_copies = [
        pltpu.make_async_copy(heat, packed.at[pl.ds(near, width * heat_rows)], in_sems.at[3, 0]),
        pltpu.make_async_copy(ends.at[0, pl.ds(0, near)], packed.at[pl.ds(0, near)], in_sems.at[3, 1]),
        pltpu.make_async_copy(
            ends.at[1, pl.ds(0, near)], packed.at[pl.ds(near + width * heat_rows, near)], in_sems.at[3, 2]
        ),
    ]
    for copy in plane_copies + heat_copies:
        copy.start()
    low_copy.start()
    for k in range(chunks):
        own_copy(k).start()
        side_copy(k).start()
    high_copy.start()

    zero = jnp.zeros((8, a.shape[-1]), jnp.float32)
    for f in range(fields_n):
        for j in range(tiles):
            b[f, HALO - 1, pl.ds(8 * j, 8)] = zero
            b[f, HALO + width, pl.ds(8 * j, 8)] = zero
    row = lax.broadcasted_iota(jnp.int32, zero.shape, 0)
    lane = lax.broadcasted_iota(jnp.int32, zero.shape, 1)
    depth = zero.shape[1]
    for copy in heat_copies:
        copy.wait()

    def unpack(i, carry):
        quarter = depth // 4
        for n in range(CHUNK):
            x = i * CHUNK + n
            for half in range(rows // 32):
                block = packed[pl.ds(x * heat_rows + 8 * half, 8)]
                for q in range(4):
                    part = pltpu.roll(block, depth - q * quarter, 1) if q else block
                    src[x, pl.ds(q * (rows // 4) + 8 * half, 8)] = jnp.where(lane < quarter, part, 0.0)
            src[x, pl.ds(rows, 8)] = packed[pl.ds(x * heat_rows + rows // 4, 8)]
        return carry

    lax.fori_loop(0, total // CHUNK, unpack, 0)
    for copy in plane_copies:
        copy.wait()
    for s in range(3):
        for r in range(fields_n * tiles):
            rec[s, pl.ds(8 * r, 8)] = 0.05 * rec[s, pl.ds(8 * r, 8)]
    low_copy.wait()

    first_row = row == 0
    final_row = row == 7
    up = jnp.where(lane == depth - 1, 0.0, 1.0).astype(jnp.float32)
    down = jnp.where(lane == 0, 0.0, 1.0).astype(jnp.float32)
    after = (row < 4) & (gy < last_gy)
    before = (row >= 4) & (gy > 0)
    side_mask = jnp.where(after | before, 1.0, 0.0).astype(jnp.float32)

    def planes_step(old, new, x, slots, last):
        count = tiles - 1 if last else tiles
        for j in range(count):
            here = pl.ds(8 * j, 8)
            above = pl.ds(8 * ((j + 1) % tiles), 8)
            below = pl.ds(8 * ((j - 1) % tiles), 8)
            columns = [[old[f, x + n, here] for n in range(-1, GROUP + 1)] for f in range(fields_n)]
            for n in range(GROUP):
                at = n + 1
                u = 0.05 * columns[2][at]
                v = 0.05 * columns[3][at]
                w = 0.05 * columns[4][at]
                c_xp, c_xm = 0.02 - u, 0.02 + u
                c_yp, c_ym = 0.02 - v, 0.02 + v
                c_zp, c_zm = up * (0.02 - w), down * (0.02 + w)
                for f in range(fields_n):
                    c = columns[f][at]
                    if j < tiles - 1:
                        yp = old[f, x + n, pl.ds(8 * j + 1, 8)]
                    else:
                        yp = jnp.where(final_row, pltpu.roll(old[f, x + n, above], 7, 0), pltpu.roll(c, 7, 0))
                    if j > 0:
                        ym = old[f, x + n, pl.ds(8 * j - 1, 8)]
                    else:
                        ym = jnp.where(first_row, pltpu.roll(old[f, x + n, below], 1, 0), pltpu.roll(c, 1, 0))
                    t1 = 0.83 * c + rec[slots[n], pl.ds(8 * (f * tiles + j), 8)]
                    t2 = c_xp * columns[f][at + 1] + c_xm * columns[f][at - 1]
                    t3 = c_yp * yp + c_ym * ym
                    t4 = c_zp * pltpu.roll(c, depth - 1, 1) + c_zm * pltpu.roll(c, 1, 1)
                    value = (t1 + t2) + (t3 + t4)
                    if f == 0:
                        value = value + src[x + n, here]
                    if j == tiles - 1:
                        value = value * side_mask
                    new[f, x + n, here] = value

    own_copy(0).wait()
    side_copy(0).wait()
    for step in range(1, STEPS + 1):
        old, new = (a, b) if step % 2 == 1 else (b, a)
        first = jnp.where(gx == 0, HALO, step)
        end = jnp.where(gx == last_gx, HALO + width, total - step)

        def body(i, carry, old=old, new=new, step=step, first=first, end=end):
            x = jnp.minimum(first + GROUP * i, end - GROUP)
            if step == 1:
                part = lax.div(x + GROUP - HALO + CHUNK, CHUNK) - 1
                past = lax.div(first + GROUP * i - HALO + CHUNK, CHUNK) - 1

                @pl.when((part > past) & (part > 0) & (part < chunks))
                def _():
                    own_copy(part).wait()
                    side_copy(part).wait()

                @pl.when((part > past) & (part == chunks))
                def _():
                    high_copy.wait()

            def slot(n):
                if step == STEPS:
                    return 1
                return jnp.where(x + n < HALO, 0, jnp.where(x + n < HALO + width, 1, 2))

            planes_step(old, new, x, [slot(n) for n in range(GROUP)], step == STEPS)
            if step == STEPS:
                done = x + GROUP - HALO

                @pl.when(lax.rem(done, CHUNK) == 0)
                def _():
                    out_copy(lax.div(done, CHUNK) - 1).start()

            return carry

        lax.fori_loop(0, lax.div(end - first + GROUP - 1, GROUP), body, 0)
    for k in range(chunks):
        out_copy(k).wait()


def stencil(fields, yside, xlow, xhigh, plane, heat, ends):
    count, width, rows, depth = fields.shape
    total = width + 2 * HALO
    buffer = pltpu.VMEM((count, total, rows + 8, depth), jnp.float32)
    return pl.pallas_call(
        functools.partial(stencil_kernel, width=width, rows=rows),
        out_shape=jax.ShapeDtypeStruct(fields.shape, jnp.float32),
        in_specs=[pl.BlockSpec(memory_space=pl.ANY)] * 7,
        out_specs=pl.BlockSpec(memory_space=pl.ANY),
        scratch_shapes=[
            buffer,
            buffer,
            pltpu.VMEM((3, count * (rows + 8), depth), jnp.float32),
            pltpu.VMEM((total * (rows // 4 + 8), depth), jnp.float32),
            pltpu.VMEM((total, rows + 8, depth), jnp.float32),
            pltpu.SemaphoreType.DMA((4, max(width // CHUNK, 5))),
            pltpu.SemaphoreType.DMA((width // CHUNK,)),
        ],
        compiler_params=pltpu.CompilerParams(vmem_limit_bytes=48 * 1024 * 1024),
        cost_estimate=pl.CostEstimate(flops=160_000_000, bytes_accessed=20_000_000, transcendentals=0),
        name="stencil",
    )(fields, yside, xlow, xhigh, plane, heat, ends)


NT = (((1,), (1,)), ((), ()))
PAIR_CHUNK = 8


def split(value):
    high = value.astype(jnp.bfloat16)
    return high, (value - high.astype(jnp.float32)).astype(jnp.bfloat16)


def live_faces(counts, t, shape):
    lane = lax.broadcasted_iota(jnp.int32, shape, 1)
    return jnp.where(lane < counts[0, t], 1.0, 0.0).astype(jnp.float32)


def summed(arrived, block, blocks):
    total = arrived[block]
    for g in range(1, arrived.shape[0] // blocks):
        total = total + arrived[g * blocks + block]
    return total


def flux_kernel(counts, emission, albedo, factors, *rest, devices, last):
    arrived, (out, held, lhs, sems) = (rest[0] if last else None), rest[-4:]
    tiles, bands, faces = emission.shape
    pairs = factors.shape[0]
    chunks = pairs // PAIR_CHUNK
    blocks = out.shape[0] // devices

    def chunk_copy(k):
        part = pl.ds(k * PAIR_CHUNK, PAIR_CHUNK)
        return pltpu.make_async_copy(factors.at[part], held.at[part], sems.at[k])

    for k in range(chunks):
        chunk_copy(k).start()
    out[...] = jnp.zeros_like(out)
    for t in range(tiles):
        radiosity = emission[t]
        if last:
            radiosity = radiosity + albedo[pl.ds(t, 1), :] * summed(arrived, t, tiles)
        radiosity = live_faces(counts, t, (bands, faces)) * radiosity
        high, low = split(radiosity)
        high, low = high.astype(jnp.float32), low.astype(jnp.float32)
        nothing = jnp.zeros_like(high)
        left = jnp.concatenate([high, low, nothing, nothing], axis=0)
        right = jnp.concatenate([high, nothing, nothing, nothing], axis=0)
        lhs[t] = jnp.concatenate([left, right], axis=1).astype(jnp.bfloat16)

    def chunk_step(k, carry):
        chunk_copy(k).wait()
        for i in range(PAIR_CHUNK // 2):
            first = k * PAIR_CHUNK + 2 * i
            both = held[pl.ds(first, 2)].reshape(2 * faces, faces)
            rhs = jnp.concatenate(split(both), axis=1)
            rows = [lhs[counts[0, tiles + first + n]] for n in range(2)]
            got = lax.dot_general(jnp.concatenate(rows, axis=0), rhs, NT, preferred_element_type=jnp.float32)
            for n in range(2):
                part = got[16 * n : 16 * n + 8, n * faces : (n + 1) * faces]
                flux = part[:bands] + part[bands : 2 * bands]
                target = counts[0, tiles + pairs + first + n]
                if last:
                    target = lax.div(target, tiles) * blocks + lax.rem(target, tiles)
                out[target] = out[target] + jnp.where(first + n < counts[0, tiles + 2 * pairs], flux, 0.0)
        return carry

    lax.fori_loop(0, chunks, chunk_step, 0)
    if last:
        groups = tiles // bands
        for e in range(devices):
            for q in range(groups):
                sums = [
                    jnp.sum(out[e * blocks + q * bands + n], axis=0, keepdims=True) for n in range(bands)
                ]
                sums = jnp.concatenate(sums, axis=0)
                if e + 1 < devices:
                    out[(e + 1) * blocks + tiles + q] = sums
                if e > 0:
                    out[(e - 1) * blocks + tiles + groups + q] = sums


def flux(counts, emission, albedo, factors, devices, arrived=None):
    tiles, bands, faces = emission.shape
    pairs = factors.shape[0]
    last = arrived is not None
    blocks = tiles + (2 * tiles // bands if last else 0)
    vector = pl.BlockSpec(memory_space=pltpu.VMEM)
    return pl.pallas_call(
        functools.partial(flux_kernel, devices=devices, last=last),
        out_shape=jax.ShapeDtypeStruct((devices * blocks, bands, faces), jnp.float32),
        in_specs=[pl.BlockSpec(memory_space=pltpu.SMEM), vector, vector, pl.BlockSpec(memory_space=pl.ANY)]
        + [vector] * last,
        out_specs=vector,
        scratch_shapes=[
            pltpu.VMEM(factors.shape, jnp.float32),
            pltpu.VMEM((tiles, 16, 2 * faces), jnp.bfloat16),
            pltpu.SemaphoreType.DMA((pairs // PAIR_CHUNK,)),
        ],
        compiler_params=pltpu.CompilerParams(vmem_limit_bytes=60 * 1024 * 1024),
        cost_estimate=pl.CostEstimate(flops=1000, bytes_accessed=1000, transcendentals=0),
        name="flux",
    )(counts, emission, albedo, factors, *([arrived] if last else []))


def one_hot(count, index):
    at = lax.broadcasted_iota(jnp.int32, (count, index.shape[1]), 0) == index
    return at


def weighed(count, index, value):
    at = one_hot(count, index)
    top = value.astype(jnp.bfloat16).astype(jnp.float32)
    both = [jnp.where(at, top, 0.0), jnp.where(at, value - top, 0.0)]
    return jnp.concatenate(both, axis=0).astype(jnp.bfloat16)


def picked(count, index):
    return jnp.where(one_hot(count, index), 1.0, 0.0).astype(jnp.bfloat16)


def heat_kernel(
    counts, emission, albedo, cells, after, before, arrived, radiosity, heat, *, width, rows, depth
):
    tiles, bands, faces = emission.shape
    quarter = depth // 4
    near = rows // 4
    blocks = tiles + 2 * tiles // bands
    level_bits = depth.bit_length() - 1
    row_bits = rows.bit_length() - 1

    def place(cell):
        return cell >> (level_bits + row_bits), (cell >> level_bits) & (rows - 1), cell & (depth - 1)

    picks, weights = [], []
    for t in range(tiles):
        live = live_faces(counts, t, (bands, faces))
        incoming = summed(arrived, t, blocks)
        share = albedo[pl.ds(t, 1), :]
        radiosity[t] = live * (emission[t] + share * incoming)
        absorbed = 0.1 * live[:1] * (1.0 - share) * jnp.sum(incoming, axis=0, keepdims=True)
        x, y, level = place(cells[pl.ds(t, 1), :])
        picks.append(picked(width * near, x * near + (y & (near - 1))))
        weights.append(weighed(depth, (y // near) * quarter + level, absorbed))
    got = lax.dot_general(
        jnp.concatenate(picks, axis=1), jnp.concatenate(weights, axis=1), NT, preferred_element_type=jnp.float32
    )
    got = got[:, :depth] + got[:, depth:]

    picks, weights = [], []
    groups = tiles // bands
    for side, about in enumerate((before, after)):
        for q in range(groups):
            incoming = summed(arrived, tiles + side * groups + q, blocks)
            absorbed = about[q] * incoming
            cell = about[groups + q].astype(jnp.int32)
            for n in range(bands):
                x, y, level = place(cell[n : n + 1])
                if side:
                    row = jnp.where(y < HALO, x * 8 + y, -1)
                else:
                    row = jnp.where(y >= rows - HALO, x * 8 + HALO + y - (rows - HALO), -1)
                picks.append(picked(width * 8, row))
                weights.append(weighed(quarter, level, absorbed[n : n + 1]))
    sides = lax.dot_general(
        jnp.concatenate(picks, axis=1), jnp.concatenate(weights, axis=1), NT, preferred_element_type=jnp.float32
    )
    sides = sides[:, :quarter] + sides[:, quarter:]
    sides = jnp.concatenate([sides, jnp.zeros((width * 8, depth - quarter), jnp.float32)], axis=1)
    for x in range(width):
        heat[pl.ds(x * (near + 8), near)] = got[x * near : (x + 1) * near]
        heat[pl.ds(x * (near + 8) + near, 8)] = sides[8 * x : 8 * x + 8]


def heating(counts, emission, albedo, cells, after, before, arrived, width, rows, depth):
    vector = pl.BlockSpec(memory_space=pltpu.VMEM)
    return pl.pallas_call(
        functools.partial(heat_kernel, width=width, rows=rows, depth=depth),
        out_shape=(
            jax.ShapeDtypeStruct(emission.shape, jnp.float32),
            jax.ShapeDtypeStruct((width * (rows // 4 + 8), depth), jnp.float32),
        ),
        in_specs=[pl.BlockSpec(memory_space=pltpu.SMEM)] + [vector] * 6,
        out_specs=(vector,) * 2,
        compiler_params=pltpu.CompilerParams(vmem_limit_bytes=32 * 1024 * 1024),
        cost_estimate=pl.CostEstimate(flops=1000, bytes_accessed=1000, transcendentals=0),
        name="heating",
    )(counts, emission, albedo, cells, after, before, arrived)


def local(
    fields,
    emission,
    albedo,
    tile_faces,
    face_cell,
    src_tile,
    dst_tile,
    view_factor,
    pair_count,
    plane_index,
):
    width = fields.shape[1]
    rows = fields.shape[2]
    depth = fields.shape[3]
    n_gx = lax.axis_size("gx")
    n_gy = lax.axis_size("gy")

    counts = jnp.concatenate([tile_faces, src_tile, dst_tile, pair_count], axis=1)
    own = counts, emission[0], albedo[0]
    bands, faces = emission.shape[2:]
    live = (jnp.arange(faces, dtype=jnp.int32) < tile_faces[0][:, None]).astype(jnp.float32)
    about = jnp.concatenate([0.1 * live * (1.0 - albedo[0]), face_cell[0].astype(jnp.float32)], axis=0)
    about = about.reshape(-1, HALO, faces)

    def side(start):
        edge = fields[:, :, start : start + HALO].reshape(-1, HALO, depth)
        return jnp.concatenate([edge, about], axis=0)

    after = shifted(side(0), "gy", -1)
    before = shifted(side(rows - HALO), "gy", 1)
    count = fields.shape[0] * width
    yside = jnp.concatenate([after[:count], before[:count]], axis=1).reshape(-1, width, 2 * HALO, depth)
    about = after[count:], before[count:]

    outgoing = flux(*own, view_factor[0], n_gy)
    arrived = lax.all_to_all(outgoing, "gy", split_axis=0, concat_axis=0, tiled=True)

    def slab(start):
        part = slice(start, start + HALO)
        return jnp.concatenate([fields[:, part], yside[:, part]], axis=2)

    plane = jnp.concatenate(
        [
            lax.dynamic_index_in_dim(fields, plane_index[0], 1, keepdims=False),
            lax.dynamic_index_in_dim(yside, plane_index[0], 1, keepdims=False),
        ],
        axis=1,
    )
    low, high = slab(0), slab(width - HALO)
    arrived, plane, low, high = lax.optimization_barrier((arrived, plane, low, high))
    plane = shifted(plane, "gx", n_gx // 2, wrap=True).reshape(-1, depth)
    xlow = shifted(high, "gx", 1)
    xhigh = shifted(low, "gx", -1)

    outgoing = flux(*own, view_factor[0], n_gy, arrived)
    outgoing, plane = lax.optimization_barrier((outgoing, plane))
    arrived = lax.all_to_all(outgoing, "gy", split_axis=0, concat_axis=0, tiled=True)
    radiosity, heat = heating(*own, face_cell[0], *about, arrived, width, rows, depth)
    near = HALO * (rows // 4 + 8)
    ends = jnp.stack(
        [
            shifted(jnp.concatenate([heat[heat.shape[0] - near :], plane], axis=0), "gx", 1),
            shifted(jnp.concatenate([heat[:near], plane], axis=0), "gx", -1),
        ]
    )
    stepped = stencil(fields, yside, xlow, xhigh, plane, heat, ends)
    return (stepped, radiosity[None])


def solution(mesh):
    return jax.shard_map(
        local,
        mesh=mesh,
        in_specs=(
            P(None, "gx", "gy", None),
            P("gx", "gy", None, None),
            P("gx", "gy", None),
            P("gx", "gy"),
            P("gx", "gy", None),
            P("gx", "gy"),
            P("gx", "gy"),
            P("gx", "gy", None, None),
            P("gx", "gy"),
            P("gx"),
        ),
        out_specs=(P(None, "gx", "gy", None), P("gx", "gy", None, None)),
        check_vma=False,
    )
```

time: 117 us -> 102 us (0.87)
  the two profiles are of different devices: /device:TPU:40 before, /device:TPU:14 now
where the time goes in v1:
time: 102 us; the launch traced here: 101 us
  Pallas kernels  43 us (42%)
  starting transfers between devices  31.1 us (30%)
  waiting for transfers between devices  14 us (14%)
  local copies, waits for them, and re-layouts  6.32 us (6%)
  other arithmetic  4.64 us (5%)
  between operations  2.17 us (2%)
    pallas_call x1, Pallas kernels, stencil(): pl.pallas_call(functools.partial(stencil_kernel, width=width, rows=rows),...  30 us
    ppermute x7, starting transfers between devices, shifted(): return lax.ppermute(value, axis, pairs)  20.7 us
    ppermute x7, waiting for transfers between devices, shifted(): return lax.ppermute(value, axis, pairs)  13.1 us
    all_to_all x2, starting transfers between devices, local(): lax.all_to_all(outgoing, 'gy', split_axis=0, concat_axis=0, tiled=True)  10.4 us
    pallas_call x2, Pallas kernels, flux(): pl.pallas_call(functools.partial(flux_kernel, devices=devices, last=last)...  10 us
    pallas_call x1, Pallas kernels, heating(): pl.pallas_call(functools.partial(heat_kernel, width=width, rows=rows, dep...  2.93 us
  transfers between devices with their start and end apart: 9, of which 4 were waited for; matrix products, arithmetic and copies ran while one was open for 7% of the time, Pallas kernels for 13%

profile of v1, /device:TPU:14, one launch (start us, length us, event | category | flops | bytes accessed | tf_op | source)
XLA Modules:
  0.0 101.3 jit_solution(9705810251440357539)
XLA Ops:
  1.3 1.7 %fusion.1 = (f32[5,48,4,128]{3,2,1,0:T(4,128)S(1)}, f32[5,48,4,128]{3,2,1,0:T(4,128)S(1)}) fusion(f32[5,48,64,128]{3,2,1,0:T(8,128)} %fields.1), kind=kLoop, calls=%fused_computation.17 | loop fusion | bytes 1966080 | tf_op jit(solution)/shard_map/slice | solution.py:438
  3.0 0.8 subtract_multiply_fusion
  4.1 1.9 %collective-permute-start = (f32[248,4,128]{2,1,0:T(4,128)S(1)}, f32[248,4,128]{2,1,0:T(4,128)S(1)}, u32[]{:S(2)}, u32[]{:S(2)}) collective-permute-start(f32[248,4,128]{2,1,0:T(4,128)S(1)} %get-tuple-element.28), channel_id=1, source_target_pairs={{1,0},{2,1},{3,2},{4,3},{5,4},{6,5},{7,6},{9,8},{10,9},{11,10},{12... | collective-permute-start | bytes 1523720 | tf_op jit(solution)/shard_map/ppermute | solution.py:20
  6.0 2.4 %collective-permute-start.1 = (f32[248,4,128]{2,1,0:T(4,128)S(1)}, f32[248,4,128]{2,1,0:T(4,128)S(1)}, u32[]{:S(2)}, u32[]{:S(2)}) collective-permute-start(f32[248,4,128]{2,1,0:T(4,128)S(1)} %get-tuple-element.29), channel_id=1, source_target_pairs={{0,1},{1,2},{2,3},{3,4},{4,5},{5,6},{6,7},{8,9},{9,10},{10,11},{11... | collective-permute-start | bytes 1523720 | tf_op jit(solution)/shard_map/ppermute | solution.py:20
  9.1 1.3 %pad_add_fusion.counts = s32[1,145]{1,0:T(1,128)} fusion(s32[1,1]{1,0:T(1,128)S(6)} %copy.12, s32[1,64]{1,0:T(1,128)} %param.16, s32[1,64]{1,0:T(1,128)} %param.15, s32[1,16]{1,0:T(1,128)} %param.13), kind=kLoop, calls=%fused_computation.14 | loop fusion | flops 435 | bytes 1160 | tf_op jit(solution)/shard_map/concatenate | solution.py:430
  10.4 4.8 %flux.2 = f32[128,4,128]{2,1,0:T(4,128)} custom-call(s32[1,145]{1,0:T(1,128)} %pad_add_fusion.counts, f32[16,4,128]{2,1,0:T(4,128)} %bitcast.28, f32[16,128]{1,0:T(8,128)} %bitcast.31, f32[64,128,128]{2,1,0:T(8,128)} %bitcast.35), custom_call_target="tpu_custom_call" | custom-call | flops 1000 | bytes 1000 | tf_op jit(solution)/shard_map/flux/pallas_call | solution.py:310
  15.2 5.6 %all-to-all-start = ((f32[128,4,128]{2,1,0:T(4,128)}), f32[128,4,128]{2,1,0:T(4,128)S(1)}, u32[]{:S(2)}, u32[]{:S(2)}) async-start(f32[128,4,128]{2,1,0:T(4,128)} %flux.2), calls=%async_computation | async-start | bytes 524288 | tf_op jit(solution)/shard_map/all_to_all | solution.py:448
  21.5 0.9 dynamic-slice_bitcast_fusion
  22.5 1.4 %fusion = (f32[5,4,64,128]{3,2,1,0:T(8,128)S(1)}, f32[5,4,64,128]{3,2,1,0:T(8,128)S(1)}) fusion(f32[5,48,64,128]{3,2,1,0:T(8,128)} %fields.1), kind=kLoop, calls=%fused_computation.16 | loop fusion | bytes 2621440 | tf_op jit(solution)/shard_map/slice | solution.py:452
  23.9 0.7 copy-done.5
  25.0 1.2 %pad_maximum_fusion.1 = (f32[5,4,72,128]{3,2,1,0:T(8,128)}, f32[5,4,72,128]{3,2,1,0:T(8,128)}) fusion(f32[5,4,8,128]{3,2,1,0:T(8,128)S(1)} %get-tuple-element.23, f32[5,4,64,128]{3,2,1,0:T(8,128)S(1)} %get-tuple-element.19, f32[5,4,8,128]{3,2,1,0:T(8,128)S(1)} %get-tuple-element.22, f32[5,4,64,128]{3,2,1,0:T(8,128)S(1)} %get-tuple-element.18), kind=kLoop, calls=%fused_computation.1 | loop fusion | flops 368640 | bytes 2949120 | tf_op jit(solution)/shard_map/concatenate | solution.py:452
  26.9 3.9 %collective-permute-start.4 = (f32[5,72,128]{2,1,0:T(8,128)S(1)}, f32[5,72,128]{2,1,0:T(8,128)S(1)}, u32[]{:S(2)}, u32[]{:S(2)}) collective-permute-start(f32[5,72,128]{2,1,0:T(8,128)S(1)} %pad_maximum_fusion.8), channel_id=1, source_target_pairs={{0,64},{8,72},{16,80},{24,88},{32,96},{40,104},{48,112},{56,120},{... | collective-permute-start | bytes 552968 | tf_op jit(solution)/shard_map/ppermute | solution.py:20
  30.8 5.2 %flux.3 = f32[192,4,128]{2,1,0:T(4,128)} custom-call(s32[1,145]{1,0:T(1,128)} %pad_add_fusion.counts, f32[16,4,128]{2,1,0:T(4,128)} %bitcast.29, f32[16,128]{1,0:T(8,128)} %bitcast.32, f32[64,128,128]{2,1,0:T(8,128)} %bitcast.36, f32[128,4,128]{2,1,0:T(4,128)} %copy-done.4), custom_call_target="tpu_custom_call" | custom-call | flops 1000 | bytes 1000 | tf_op jit(solution)/shard_map/flux/pallas_call | solution.py:310
  36.0 4.8 %all-to-all-start.1 = ((f32[192,4,128]{2,1,0:T(4,128)}), f32[192,4,128]{2,1,0:T(4,128)S(1)}, u32[]{:S(2)}, u32[]{:S(2)}) async-start(f32[192,4,128]{2,1,0:T(4,128)} %flux.3), calls=%async_computation.1 | async-start | bytes 786432 | tf_op jit(solution)/shard_map/all_to_all | solution.py:469
  40.9 2.8 %collective-permute-start.2 = (f32[5,4,72,128]{3,2,1,0:T(8,128)}, f32[5,4,72,128]{3,2,1,0:T(8,128)S(1)}, u32[]{:S(2)}, u32[]{:S(2)}) collective-permute-start(f32[5,4,72,128]{3,2,1,0:T(8,128)} %get-tuple-element.10), channel_id=1, source_target_pairs={{0,8},{8,16},{16,24},{24,32},{32,40},{40,48},{48,56},{56,64},{64,7... | collective-permute-start | bytes 2211848 | tf_op jit(solution)/shard_map/ppermute | solution.py:20
  43.7 3.0 %collective-permute-start.3 = (f32[5,4,72,128]{3,2,1,0:T(8,128)}, f32[5,4,72,128]{3,2,1,0:T(8,128)S(1)}, u32[]{:S(2)}, u32[]{:S(2)}) collective-permute-start(f32[5,4,72,128]{3,2,1,0:T(8,128)} %get-tuple-element.11), channel_id=1, source_target_pairs={{8,0},{16,8},{24,16},{32,24},{40,32},{48,40},{56,48},{64,56},{72,6... | collective-permute-start | bytes 2211848 | tf_op jit(solution)/shard_map/ppermute | solution.py:20
  46.7 0.7 slice.52.after
  47.4 0.7 slice.53.before
  48.4 2.9 %heating.1 = (f32[16,4,128]{2,1,0:T(4,128)}, f32[1152,128]{1,0:T(8,128)S(1)}) custom-call(s32[1,145]{1,0:T(1,128)S(1)} %copy-done.3, f32[16,4,128]{2,1,0:T(4,128)S(1)} %bitcast.30, f32[16,128]{1,0:T(8,128)S(1)} %bitcast.33, s32[16,128]{1,0:T(8,128)S(1)} %bitcast.34, f32[8,4,128]{2,1,0:T(4,128)S(1)} %slice.52.after, f32[8,4,128]{2,1,0:T(4,128)S(1)} %slice.53.before, ...), custom_call_target="tpu_custom_call" | custom-call | flops 1000 | bytes 1000 | tf_op jit(solution)/shard_map/heating/pallas_call | solution.py:398
  51.4 4.7 %collective-permute-start.5 = (f32[456,128]{1,0:T(8,128)S(1)}, f32[456,128]{1,0:T(8,128)S(1)}, u32[]{:S(2)}, u32[]{:S(2)}) collective-permute-start(f32[456,128]{1,0:T(8,128)S(1)} %get-tuple-element.26), channel_id=1, source_target_pairs={{0,8},{8,16},{16,24},{24,32},{32,40},{40,48},{48,56},{56,64},{64,7... | collective-permute-start | bytes 700424 | tf_op jit(solution)/shard_map/ppermute | solution.py:20
  56.1 1.9 %collective-permute-start.6 = (f32[456,128]{1,0:T(8,128)S(1)}, f32[456,128]{1,0:T(8,128)S(1)}, u32[]{:S(2)}, u32[]{:S(2)}) collective-permute-start(f32[456,128]{1,0:T(8,128)S(1)} %get-tuple-element.27), channel_id=1, source_target_pairs={{8,0},{16,8},{24,16},{32,24},{40,32},{48,40},{56,48},{64,56},{72,6... | collective-permute-start | bytes 700424 | tf_op jit(solution)/shard_map/ppermute | solution.py:20
  58.1 8.4 %collective-permute-done.5 = f32[456,128]{1,0:T(8,128)S(1)} collective-permute-done((f32[456,128]{1,0:T(8,128)S(1)}, f32[456,128]{1,0:T(8,128)S(1)}, u32[]{:S(2)}, u32[]{:S(2)}) %collective-permute-start.5) | collective-permute-done | bytes 233504 | tf_op jit(solution)/shard_map/ppermute | solution.py:20
  66.5 4.7 %collective-permute-done.6 = f32[456,128]{1,0:T(8,128)S(1)} collective-permute-done((f32[456,128]{1,0:T(8,128)S(1)}, f32[456,128]{1,0:T(8,128)S(1)}, u32[]{:S(2)}, u32[]{:S(2)}) %collective-permute-start.6) | collective-permute-done | bytes 233504 | tf_op jit(solution)/shard_map/ppermute | solution.py:20
  71.3 30.0 %stencil.1 = f32[5,48,64,128]{3,2,1,0:T(8,128)} custom-call(f32[5,48,64,128]{3,2,1,0:T(8,128)} %fields.1, f32[5,48,8,128]{3,2,1,0:T(8,128)S(1)} %bitcast.25, f32[5,4,72,128]{3,2,1,0:T(8,128)S(1)} %collective-permute-done.2.xlow, f32[5,4,72,128]{3,2,1,0:T(8,128)S(1)} %collective-permute-done.3.xhigh, f32[360,128]{1,0:T(8,128)S(1)} %bitcast.27, ...), custom_call_target="tpu_custom_call" | custom-call | flops 160000000 | bytes 20000000 | tf_op jit(solution)/shard_map/stencil/pallas_call | solution.py:205
  (32 shorter events, 2.3 us)
Async XLA Ops:
  4.1 19.8 %collective-permute-start = (f32[248,4,128]{2,1,0:T(4,128)S(1)}, f32[248,4,128]{2,1,0:T(4,128)S(1)}, u32[]{:S(2)}, u32[]{:S(2)}) collective-permute-start(f32[248,4,128]{2,1,0:T(4,128)S(1)} %get-tuple-element.28), channel_id=1, source_target_pairs={{1,0},{2,1},{3,2},{4,3},{5,4},{6,5},{7,6},{9,8},{10,9},{11,10},{12... | collective-permute-start | bytes 1523720 | tf_op jit(solution)/shard_map/ppermute | solution.py:20
  6.0 17.9 %collective-permute-start.1 = (f32[248,4,128]{2,1,0:T(4,128)S(1)}, f32[248,4,128]{2,1,0:T(4,128)S(1)}, u32[]{:S(2)}, u32[]{:S(2)}) collective-permute-start(f32[248,4,128]{2,1,0:T(4,128)S(1)} %get-tuple-element.29), channel_id=1, source_target_pairs={{0,1},{1,2},{2,3},{3,4},{4,5},{5,6},{6,7},{8,9},{9,10},{10,11},{11... | collective-permute-start | bytes 1523720 | tf_op jit(solution)/shard_map/ppermute | solution.py:20
  15.2 11.7 %all-to-all-start = ((f32[128,4,128]{2,1,0:T(4,128)}), f32[128,4,128]{2,1,0:T(4,128)S(1)}, u32[]{:S(2)}, u32[]{:S(2)}) async-start(f32[128,4,128]{2,1,0:T(4,128)} %flux.2), calls=%async_computation | async-start | bytes 524288 | tf_op jit(solution)/shard_map/all_to_all | solution.py:448
  22.4 26.0 %copy-start = (f32[1,16,4,128]{3,2,1,0:T(4,128)S(1)}, f32[1,16,4,128]{3,2,1,0:T(4,128)}, u32[]{:S(2)}) copy-start(f32[1,16,4,128]{3,2,1,0:T(4,128)} %param.11) | copy-start | bytes 98308
  22.4 26.0 %copy-start.1 = (f32[1,16,128]{2,1,0:T(8,128)S(1)}, f32[1,16,128]{2,1,0:T(8,128)}, u32[]{:S(2)}) copy-start(f32[1,16,128]{2,1,0:T(8,128)} %param.12) | copy-start | bytes 24580
  22.4 25.9 %copy-start.2 = (s32[1,16,128]{2,1,0:T(8,128)S(1)}, s32[1,16,128]{2,1,0:T(8,128)}, u32[]{:S(2)}) copy-start(s32[1,16,128]{2,1,0:T(8,128)} %param.14) | copy-start | bytes 24580
  22.5 25.9 %copy-start.3 = (s32[1,145]{1,0:T(1,128)S(1)}, s32[1,145]{1,0:T(1,128)}, u32[]{:S(2)}) copy-start(s32[1,145]{1,0:T(1,128)} %pad_add_fusion.counts) | copy-start | bytes 1744
  23.9 0.8 copy-start.5
  24.7 11.3 %copy-start.6 = (f32[248,4,128]{2,1,0:T(4,128)}, f32[248,4,128]{2,1,0:T(4,128)S(1)}, u32[]{:S(2)}) copy-start(f32[248,4,128]{2,1,0:T(4,128)S(1)} %collective-permute-done.1) | copy-start | bytes 1523716
  26.9 3.9 %copy-start.4 = (f32[128,4,128]{2,1,0:T(4,128)}, f32[128,4,128]{2,1,0:T(4,128)S(1)}, u32[]{:S(2)}) copy-start(f32[128,4,128]{2,1,0:T(4,128)S(1)} %all-to-all-done.rest_0_) | copy-start | bytes 786436
  26.9 9.1 %collective-permute-start.4 = (f32[5,72,128]{2,1,0:T(8,128)S(1)}, f32[5,72,128]{2,1,0:T(8,128)S(1)}, u32[]{:S(2)}, u32[]{:S(2)}) collective-permute-start(f32[5,72,128]{2,1,0:T(8,128)S(1)} %pad_maximum_fusion.8), channel_id=1, source_target_pairs={{0,64},{8,72},{16,80},{24,88},{32,96},{40,104},{48,112},{56,120},{... | collective-permute-start | bytes 552968 | tf_op jit(solution)/shard_map/ppermute | solution.py:20
  36.0 12.3 %all-to-all-start.1 = ((f32[192,4,128]{2,1,0:T(4,128)}), f32[192,4,128]{2,1,0:T(4,128)S(1)}, u32[]{:S(2)}, u32[]{:S(2)}) async-start(f32[192,4,128]{2,1,0:T(4,128)} %flux.3), calls=%async_computation.1 | async-start | bytes 786432 | tf_op jit(solution)/shard_map/all_to_all | solution.py:469
  40.9 30.4 %collective-permute-start.2 = (f32[5,4,72,128]{3,2,1,0:T(8,128)}, f32[5,4,72,128]{3,2,1,0:T(8,128)S(1)}, u32[]{:S(2)}, u32[]{:S(2)}) collective-permute-start(f32[5,4,72,128]{3,2,1,0:T(8,128)} %get-tuple-element.10), channel_id=1, source_target_pairs={{0,8},{8,16},{16,24},{24,32},{32,40},{40,48},{48,56},{56,64},{64,7... | collective-permute-start | bytes 2211848 | tf_op jit(solution)/shard_map/ppermute | solution.py:20
  43.7 27.5 %collective-permute-start.3 = (f32[5,4,72,128]{3,2,1,0:T(8,128)}, f32[5,4,72,128]{3,2,1,0:T(8,128)S(1)}, u32[]{:S(2)}, u32[]{:S(2)}) collective-permute-start(f32[5,4,72,128]{3,2,1,0:T(8,128)} %get-tuple-element.11), channel_id=1, source_target_pairs={{8,0},{16,8},{24,16},{32,24},{40,32},{48,40},{56,48},{64,56},{72,6... | collective-permute-start | bytes 2211848 | tf_op jit(solution)/shard_map/ppermute | solution.py:20
  51.4 15.1 %collective-permute-start.5 = (f32[456,128]{1,0:T(8,128)S(1)}, f32[456,128]{1,0:T(8,128)S(1)}, u32[]{:S(2)}, u32[]{:S(2)}) collective-permute-start(f32[456,128]{1,0:T(8,128)S(1)} %get-tuple-element.26), channel_id=1, source_target_pairs={{0,8},{8,16},{16,24},{24,32},{32,40},{40,48},{48,56},{56,64},{64,7... | collective-permute-start | bytes 700424 | tf_op jit(solution)/shard_map/ppermute | solution.py:20
  56.1 15.1 %collective-permute-start.6 = (f32[456,128]{1,0:T(8,128)S(1)}, f32[456,128]{1,0:T(8,128)S(1)}, u32[]{:S(2)}, u32[]{:S(2)}) collective-permute-start(f32[456,128]{1,0:T(8,128)S(1)} %get-tuple-element.27), channel_id=1, source_target_pairs={{8,0},{16,8},{24,16},{32,24},{40,32},{48,40},{56,48},{64,56},{72,6... | collective-permute-start | bytes 700424 | tf_op jit(solution)/shard_map/ppermute | solution.py:20
